TPU v7x, 256 devices: a whole 4x4x8 slice. The times are simulated.
256 devices in a mesh: slab: 32 (over y, x, core), coil: 8 (over z).
Axes of the slice: x: 4, y: 4, z: 8, core: 2. Of those that a mesh axis runs over, the one named last changes fastest.
Arguments:
- image_est: bfloat16 [2, 256, 256, 256], P(None, 'slab', 'coil'), may hold values from -6 to 6
- coil_maps: bfloat16 [8, 2, 256, 256, 256], P('coil', None, 'slab'), may hold values from -6 to 6
- kernel_tiles: bfloat16 [5120, 128, 256], P('slab'), may hold values from -0.375 to 0.375
- tile_ids: int32 [5120], P('slab'), may hold values from 0 to 2047, as said below
- tile_count: int32 [32], P('slab'), may hold values from 1 to 160, as said below
- measured: float32 [8, 2, 5120, 128], P('coil', None, 'slab'), may hold values from -6 to 6
Outputs:
- residual: float32 [8, 2, 5120, 128], P('coil', None, 'slab')
- rms: float32 [1], replicated
Inputs may be any that keep to these rules, and one draw needn't show every extreme that they name: The live slots of a slab are its first tile_count slots; some slab has all 160 live. `tile_ids`: the slots of one slab read distinct tiles.
All inputs are finite; a program needn't handle non-finite values.
Results may differ from a plain program's by a relative error of at most 0.0003.
Values may be sent and summed in bfloat16 or wider, within the bound.
A program may use at most 192 MiB of HBM per device.

v0:
```python
import jax
import jax.numpy as jnp
import ml_dtypes
import numpy as np
from jax import lax
from jax.experimental import pallas as pl
from jax.experimental.pallas import tpu as pltpu
from jax.sharding import PartitionSpec as P

F32 = jnp.float32
BF16 = jnp.bfloat16
MESH = pl.DeviceIdType.MESH

IMG = 256
KXW = 64
FREQ = 512
SLABS = 32
COILS = 8
PLANES = 8
YB = 32
LANES = 128
KZ = 16
SLOTS = 160
CHUNKS = ((0,), (1, 7), (2, 6), (3, 5), (4,))


def split_table(table):
    table = table.astype(np.float32)
    high = table.astype(ml_dtypes.bfloat16)
    low = (table - high.astype(np.float32)).astype(ml_dtypes.bfloat16)
    return high, low


def angles(rows, cols, row_offset, col_offset):
    index = (np.arange(rows)[:, None] - row_offset) * (np.arange(cols)[None, :] - col_offset)
    return (index % FREQ) * (2.0 * np.pi / FREQ)


def x_table():
    phase = angles(IMG, KXW, IMG // 2, KXW // 2)
    cosine, sine = np.cos(phase) / 4096.0, np.sin(phase) / 4096.0
    table = np.block([[cosine, -sine], [sine, cosine]])
    high, low = split_table(table)
    return np.concatenate([high, low], axis=1)


def long_table(row_offset, col_offset):
    phase = angles(FREQ, IMG, row_offset, col_offset)
    high, low = split_table(np.concatenate([np.cos(phase), np.sin(phase)], axis=1))
    return np.concatenate([high, high, low], axis=1)


def place_table():
    table = np.zeros((8, 2, 64, 2, 256), np.float32)
    for w in range(8):
        for part in range(2):
            for u in range(4):
                for v in range(8):
                    table[w, part, 8 * u + v, part, 64 * u + 8 * v + w] = 1.0
    return table.reshape(1024, 512).astype(ml_dtypes.bfloat16)


def split(value):
    high = value.astype(BF16)
    low = (value - high.astype(F32)).astype(BF16)
    return high, low


def kernel(
    img_hbm, maps_hbm, kern_hbm, ids, count, meas, tx_hbm, ez_hbm, ey_hbm, place_hbm,
    res, rms,
    img, maps, kern, tx, ez, ey, place,
    send_a, lines, send_b, planes, grid, picked, cells, sums_c, sums_s,
    load_sem, ring_send, ring_recv, a_send, a_recv, b_send, b_recv, sum_send, sum_recv,
):
    me = lax.axis_index("slab")
    coil = lax.axis_index("coil")
    left = lax.rem(coil + COILS - 1, COILS)
    right = lax.rem(coil + 1, COILS)

    def load(index, src, dst):
        copy = pltpu.make_async_copy(src, dst, load_sem.at[index])
        copy.start()
        return copy

    load_img = load(0, img_hbm, img.at[0])
    load_maps = load(1, maps_hbm.at[0], maps)
    load_tx = load(2, tx_hbm, tx)
    load_ez = load(3, ez_hbm, ez)
    load_ey = load(4, ey_hbm, ey)
    load_place = load(5, place_hbm, place)
    load_kern = load(6, kern_hbm, kern)

    barrier = pltpu.get_barrier_semaphore()

    @pl.loop(1, SLABS)
    def _(step):
        pl.semaphore_signal(
            barrier, inc=1, device_id={"slab": lax.rem(me + step, SLABS)}, device_id_type=MESH
        )

    @pl.loop(1, COILS)
    def _(step):
        pl.semaphore_signal(
            barrier, inc=1, device_id={"coil": lax.rem(coil + step, COILS)}, device_id_type=MESH
        )

    pl.semaphore_wait(barrier, SLABS - 1 + COILS - 1)

    def hop(direction, step, part):
        target = left if direction == 0 else right
        dst_slot = step if direction == 0 else 8 - step
        src_slot = (dst_slot - 1) if direction == 0 else (dst_slot + 1) % 8
        src = img_hbm.at[part] if step == 1 else img.at[src_slot, part]
        return pltpu.make_async_remote_copy(
            src_ref=src,
            dst_ref=img.at[dst_slot, part],
            send_sem=ring_send.at[direction, step - 1, part],
            recv_sem=ring_recv.at[direction, step - 1, part],
            device_id={"coil": target},
            device_id_type=MESH,
        )

    hops = {}
    for direction in range(2):
        for step in range(1, 5):
            for part in range(2):
                if step < 4 or part == direction:
                    hops[direction, step, part] = hop(direction, step, part)

    for part in range(2):
        for direction in range(2):
            hops[direction, 1, part].start()

    def arrive(step):
        for part in range(2):
            for direction in range(2):
                if (direction, step, part) in hops:
                    hops[direction, step, part].wait_recv()
                    if (direction, step + 1, part) in hops:
                        hops[direction, step + 1, part].start()

    lane = lax.broadcasted_iota(jnp.int32, (1, LANES), 1)
    sign = jnp.where(lane < 64, 1.0, -1.0).astype(F32)

    def along_x(slot, entry):
        block = lax.rem(coil + slot, COILS)
        rows = pl.ds(pl.multiple_of(block * YB, YB), YB)
        ar = img[slot, 0].astype(F32)
        ai = img[slot, 1].astype(F32)
        sr = maps[0, :, rows, :].astype(F32)
        si = maps[1, :, rows, :].astype(F32)
        wr = (ar * sr - ai * si).reshape(PLANES * YB, IMG)
        wi = (ar * si + ai * sr).reshape(PLANES * YB, IMG)
        high, low = split(jnp.concatenate([wr, wi], axis=1))
        both = jnp.dot(high, tx[...], preferred_element_type=F32)
        out = both[:, :LANES] + both[:, LANES:]
        out = out + jnp.dot(low, tx[:, :LANES], preferred_element_type=F32)
        for z in range(PLANES):
            send_a[entry, pl.ds(z, YB, stride=PLANES), :] = out[z * YB : (z + 1) * YB]

    def exchange(src, dst, chunk, width, send_sem, recv_sem):
        entries = pl.ds(2 * chunk, len(CHUNKS[chunk]))
        mine = pl.ds(pl.multiple_of(me * width, width), width)

        @pl.loop(1, SLABS)
        def _(step):
            peer = lax.rem(me + step, SLABS)
            theirs = pl.ds(pl.multiple_of(peer * width, width), width)
            pltpu.make_async_remote_copy(
                src_ref=src.at[entries, theirs],
                dst_ref=dst.at[entries, mine],
                send_sem=send_sem.at[chunk],
                recv_sem=recv_sem.at[chunk],
                device_id={"slab": peer},
                device_id_type=MESH,
            ).start()

        dst[entries, mine, :] = src[entries, mine, :]

    def wait_all(ref, chunk, width, sem):
        part = ref.at[pl.ds(2 * chunk, len(CHUNKS[chunk])), pl.ds(0, (SLABS - 1) * width)]
        pltpu.make_async_copy(part, part, sem.at[chunk]).wait()

    def turned(value):
        swapped = [
            sign * pltpu.roll(value[:, i : i + LANES], 64, 1) for i in range(0, value.shape[1], LANES)
        ]
        return jnp.concatenate([value, jnp.concatenate(swapped, axis=1)], axis=0)

    def transform(table, value):
        high, low = split(turned(value))
        return jnp.dot(
            table[...], jnp.concatenate([high, low, high], axis=0), preferred_element_type=F32
        )

    def stage_x(chunk):
        for i, slot in enumerate(CHUNKS[chunk]):
            along_x(slot, 2 * chunk + i)
        exchange(send_a, lines, chunk, PLANES, a_send, a_recv)

    def stage_z(chunk):
        wait_all(lines, chunk, PLANES, a_recv)
        count_here = len(CHUNKS[chunk])
        value = jnp.concatenate([lines[2 * chunk + i] for i in range(count_here)], axis=1)
        out = transform(ez, value)
        for i in range(count_here):
            send_b[2 * chunk + i] = out[:, i * LANES : (i + 1) * LANES]
        exchange(send_b, planes, chunk, KZ, b_send, b_recv)

    load_img.wait()
    load_maps.wait()
    load_tx.wait()
    stage_x(0)
    load_ez.wait()
    for chunk in range(1, 5):
        arrive(chunk)
        stage_x(chunk)
        stage_z(chunk - 1)
    stage_z(4)
    load_ey.wait()
    load_place.wait()
    load_kern.wait()
    for chunk in range(5):
        wait_all(planes, chunk, KZ, b_recv)

    def entry_of(block):
        slot = lax.rem(block - coil + COILS, COILS)
        return jnp.where(slot <= 4, 2 * slot, 2 * (COILS - slot) + 1)

    entries = [entry_of(block) for block in range(COILS)]

    @pl.loop(0, KZ // 2)
    def _(pair):
        halves = []
        for odd in range(2):
            halves.append(
                jnp.concatenate(
                    [planes[e, pl.ds(2 * pair + odd, SLABS, stride=KZ), :] for e in entries], axis=0
                )
            )
        out = transform(ey, jnp.concatenate(halves, axis=1))
        for odd in range(2):
            half = out[:, odd * LANES : (odd + 1) * LANES].reshape(64, 8, LANES)
            grid[pl.ds((2 * pair + odd) * 64, 64)] = half

    place_of = lax.broadcasted_iota(jnp.int32, (8, LANES), 1) // 8

    @pl.loop(0, SLOTS, unroll=4)
    def _(slot):
        tile = ids[slot]
        first = (tile >> 9) * 256 + (tile & 63)
        b = jnp.full((8, LANES), (tile >> 6) & 7, jnp.int32)
        away = (place_of - b) & 7
        total = jnp.zeros((8, LANES), F32)
        for u in range(4):
            value = grid[first + 64 * u]
            total = jnp.where(away == u, pltpu.roll(value, 8 * u, 1) if u else value, total)
        for bit in (1, 2, 4):
            total = jnp.where((b & bit) > 0, pltpu.roll(total, LANES - 8 * bit, 1), total)
        picked[pl.ds(pl.multiple_of(slot * 8, 8), 8), :] = total

    high_sum = jnp.zeros((SLOTS, 512), F32)
    low_sum = jnp.zeros((SLOTS, 512), F32)
    for w in range(8):
        high, low = split(picked[pl.ds(w, SLOTS, stride=8), :])
        spot = place[w * LANES : (w + 1) * LANES, :]
        high_sum = high_sum + jnp.dot(high, spot, preferred_element_type=F32)
        low_sum = low_sum + jnp.dot(low, spot, preferred_element_type=F32)
    cells[0] = high_sum
    cells[1] = low_sum

    live = count[0]
    row = lax.broadcasted_iota(jnp.int32, (8, LANES), 0)
    row4 = lax.rem(lax.broadcasted_iota(jnp.int32, (32, LANES), 0), 8)

    def degrid(index, squares):
        first = pl.multiple_of(index * 8, 8)
        rows = pl.ds(first, 8)
        left_side = jnp.concatenate(
            [
                cells[0, rows, :256], cells[1, rows, :256],
                cells[0, rows, 256:], cells[1, rows, 256:],
            ],
            axis=0,
        ).astype(BF16)
        total = jnp.zeros((32, LANES), F32)
        for s in range(8):
            product = lax.dot_general(
                left_side, kern[first + s], (((1,), (1,)), ((), ())), preferred_element_type=F32
            )
            total = jnp.where(row4 == s, product, total)
        alive = first + row < live
        for part in range(2):
            predicted = total[16 * part : 16 * part + 8] + total[16 * part + 8 : 16 * part + 16]
            value = jnp.where(alive, predicted - meas[0, part, rows, :], 0.0)
            res[0, part, rows, :] = value
            squares = squares + value * value
        return squares

    squares = lax.fori_loop(0, SLOTS // 8, degrid, jnp.zeros((8, LANES), F32))

    def total_over(buffer, axis, position, size, which, value):
        buffer[position] = value

        @pl.loop(1, size)
        def _(step):
            pltpu.make_async_remote_copy(
                src_ref=buffer.at[position],
                dst_ref=buffer.at[position],
                send_sem=sum_send.at[which],
                recv_sem=sum_recv.at[which],
                device_id={axis: lax.rem(position + step, size)},
                device_id_type=MESH,
            ).start()

        others = buffer.at[pl.ds(0, size - 1)]
        pltpu.make_async_copy(others, others, sum_recv.at[which]).wait()
        return jnp.sum(buffer[...], axis=0)

    squares = total_over(sums_c, "coil", coil, COILS, 0, squares)
    squares = total_over(sums_s, "slab", me, SLABS, 1, squares)
    total = jnp.sum(jnp.sum(squares, axis=1, keepdims=True), axis=0, keepdims=True)
    root = jnp.sqrt(total * (1.0 / (COILS * 2 * SLABS * SLOTS * LANES)))
    rms[...] = jnp.broadcast_to(root, (8, LANES))

    for copy in hops.values():
        copy.wait_send()
    for chunk in range(5):
        wait_all(send_a, chunk, PLANES, a_send)
        wait_all(send_b, chunk, KZ, b_send)
    for which, (buffer, size) in enumerate(((sums_c, COILS), (sums_s, SLABS))):
        others = buffer.at[pl.ds(0, size - 1)]
        pltpu.make_async_copy(others, others, sum_send.at[which]).wait()


def per_device(image_est, coil_maps, kernel_tiles, tile_ids, tile_count, measured):
    hbm = pl.BlockSpec(memory_space=pl.ANY)
    vmem = pl.BlockSpec(memory_space=pltpu.VMEM)
    smem = pl.BlockSpec(memory_space=pltpu.SMEM)
    tables = [
        jnp.asarray(x_table()),
        jnp.asarray(long_table(0, 0)),
        jnp.asarray(long_table(FREQ // 2, IMG // 2)),
        jnp.asarray(place_table()),
    ]
    residual, rms = pl.pallas_call(
        kernel,
        out_shape=(
            jax.ShapeDtypeStruct((1, 2, SLOTS, LANES), F32),
            jax.ShapeDtypeStruct((8, LANES), F32),
        ),
        in_specs=[hbm, hbm, hbm, smem, smem, vmem, hbm, hbm, hbm, hbm],
        out_specs=(vmem, vmem),
        scratch_shapes=[
            pltpu.VMEM((8, 2, PLANES, YB, IMG), BF16),
            pltpu.VMEM((2, PLANES, IMG, IMG), BF16),
            pltpu.VMEM((SLOTS, LANES, 256), BF16),
            pltpu.VMEM((2 * IMG, 2 * LANES), BF16),
            pltpu.VMEM((FREQ, 6 * IMG), BF16),
            pltpu.VMEM((FREQ, 6 * IMG), BF16),
            pltpu.VMEM((1024, 512), BF16),
            pltpu.VMEM((10, SLABS * PLANES, LANES), F32),
            pltpu.VMEM((10, SLABS * PLANES, LANES), F32),
            pltpu.VMEM((10, FREQ, LANES), F32),
            pltpu.VMEM((10, FREQ, LANES), F32),
            pltpu.VMEM((KZ * 64, 8, LANES), F32),
            pltpu.VMEM((SLOTS * 8, LANES), F32),
            pltpu.VMEM((2, SLOTS, 512), F32),
            pltpu.VMEM((COILS, 8, LANES), F32),
            pltpu.VMEM((SLABS, 8, LANES), F32),
            pltpu.SemaphoreType.DMA((7,)),
            pltpu.SemaphoreType.DMA((2, 4, 2)),
            pltpu.SemaphoreType.DMA((2, 4, 2)),
            pltpu.SemaphoreType.DMA((5,)),
            pltpu.SemaphoreType.DMA((5,)),
            pltpu.SemaphoreType.DMA((5,)),
            pltpu.SemaphoreType.DMA((5,)),
            pltpu.SemaphoreType.DMA((2,)),
            pltpu.SemaphoreType.DMA((2,)),
        ],
        compiler_params=pltpu.CompilerParams(
            collective_id=0, has_side_effects=True, vmem_limit_bytes=56 * 1024 * 1024
        ),
        cost_estimate=pl.CostEstimate(
            flops=6_000_000_000, bytes_accessed=20_000_000, transcendentals=0
        ),
    )(image_est, coil_maps, kernel_tiles, tile_ids, tile_count, measured, *tables)
    return residual, rms[0, :1]


def solution(mesh):
    placed = (
        P(None, "slab", "coil", None),
        P("coil", None, "slab", None, None),
        P("slab", None, None),
        P("slab"),
        P("slab"),
        P("coil", None, "slab", None),
    )
    return jax.shard_map(
        per_device,
        mesh=mesh,
        in_specs=placed,
        out_specs=(P("coil", None, "slab", None), P()),
        check_vma=False,
    )
```

profile of v0, /device:TPU:1, one launch (start us, length us, event | category | flops | bytes accessed | tf_op | source)
XLA Modules:
  0.0 96.9 jit_solution(5387561374101285879)
XLA Ops:
  1.3 92.9 %shard_map.113 = (f32[1,2,160,128]{3,2,1,0:T(8,128)}, f32[8,128]{1,0:T(8,128)}) custom-call(bf16[2,8,32,256]{3,2,1,0:T(8,128)(2,1)} %img_hbm.1, bf16[1,2,8,256,256]{4,3,2,1,0:T(8,128)(2,1)} %maps_hbm.1, bf16[160,128,256]{2,1,0:T(8,128)(2,1)} %kern_hbm.1, s32[160]{0:T(256)} %ids.1, s32[1]{0:T(128)S(6)} %copy.13.count, f32[1,2,160,128]{3,2,1,0:T(8,128)} %meas.1, ...), custom_call_target="tpu_custom_call" | custom-call | flops 6000000000 | bytes 20000000 | tf_op jit(solution)/shard_map/pallas_call | solution.py:347
  94.2 1.2 %slice.3 = f32[1,1]{1,0:T(1,128)} slice(f32[8,128]{1,0:T(8,128)} %get-tuple-element.5), slice={[0:1], [0:1]} | slice | bytes 8 | tf_op jit(solution)/shard_map/slice | solution.py:389
  95.4 1.6 %copy.14 = f32[1,2,160,128]{3,2,1,0:T(8,128)} copy(f32[1,2,160,128]{3,2,1,0:T(8,128)} %get-tuple-element.8) | data formatting | bytes 327680
where the time goes:
time: 97.1 us; the launch traced here: 96.9 us
  Pallas kernels  92.9 us (96%)
  local copies, waits for them, and re-layouts  2.78 us (3%)
  between operations  1.29 us (1%)
    pallas_call x1, Pallas kernels, per_device(): pl.pallas_call(kernel, out_shape=(jax.ShapeDtypeStruct((1, 2, SLOTS, LANE...  92.9 us

commit v1 on v0

--- a/solution.py
+++ b/solution.py
@@ -21,6 +21,7 @@
 LANES = 128
 KZ = 16
 SLOTS = 160
+STEPS = 32760.0
 CHUNKS = ((0,), (1, 7), (2, 6), (3, 5), (4,))
 
 
@@ -67,11 +68,13 @@
 
 
 def kernel(
-    img_hbm, maps_hbm, kern_hbm, ids, count, meas, tx_hbm, ez_hbm, ey_hbm, place_hbm,
+    img_hbm, maps_hbm, kern_hbm, ids_hbm, count_hbm, meas_hbm, tx_hbm, ez_hbm, ey_hbm, place_hbm,
     res, rms,
-    img, maps, kern, tx, ez, ey, place,
-    send_a, lines, send_b, planes, grid, picked, cells, sums_c, sums_s,
-    load_sem, ring_send, ring_recv, a_send, a_recv, b_send, b_recv, sum_send, sum_recv,
+    img, maps, kern, ids, count, meas, tx, ez, ey, place,
+    send_a, lines, send_b, planes, send_q, coded, send_s, scales, grid, picked, cells,
+    sums_c, sums_s,
+    load_sem, ring_send, ring_recv, a_send, a_recv, b_send, b_recv, s_send, s_recv,
+    sum_send, sum_recv,
 ):
     me = lax.axis_index("slab")
     coil = lax.axis_index("coil")
@@ -83,14 +86,6 @@
         copy.start()
         return copy
 
-    load_img = load(0, img_hbm, img.at[0])
-    load_maps = load(1, maps_hbm.at[0], maps)
-    load_tx = load(2, tx_hbm, tx)
-    load_ez = load(3, ez_hbm, ez)
-    load_ey = load(4, ey_hbm, ey)
-    load_place = load(5, place_hbm, place)
-    load_kern = load(6, kern_hbm, kern)
-
     barrier = pltpu.get_barrier_semaphore()
 
     @pl.loop(1, SLABS)
@@ -105,6 +100,9 @@
             barrier, inc=1, device_id={"coil": lax.rem(coil + step, COILS)}, device_id_type=MESH
         )
 
+    load_img = load(0, img_hbm, img.at[0])
+    load_maps = load(1, maps_hbm.at[0], maps)
+    load_tx = load(2, tx_hbm, tx)
     pl.semaphore_wait(barrier, SLABS - 1 + COILS - 1)
 
     def hop(direction, step, part):
@@ -131,6 +129,16 @@
     for part in range(2):
         for direction in range(2):
             hops[direction, 1, part].start()
+
+    load_ez = load(3, ez_hbm, ez)
+    late_loads = [
+        load(4, ey_hbm, ey),
+        load(5, place_hbm, place),
+        load(6, kern_hbm, kern),
+        load(7, ids_hbm, ids),
+        load(8, count_hbm, count),
+        load(9, meas_hbm.at[0], meas),
+    ]
 
     def arrive(step):
         for part in range(2):
@@ -159,8 +167,8 @@
         for z in range(PLANES):
             send_a[entry, pl.ds(z, YB, stride=PLANES), :] = out[z * YB : (z + 1) * YB]
 
-    def exchange(src, dst, chunk, width, send_sem, recv_sem):
-        entries = pl.ds(2 * chunk, len(CHUNKS[chunk]))
+    def exchange(src, dst, first, number, width, send_sem, recv_sem):
+        entries = pl.ds(first, number)
         mine = pl.ds(pl.multiple_of(me * width, width), width)
 
         @pl.loop(1, SLABS)
@@ -170,17 +178,17 @@
             pltpu.make_async_remote_copy(
                 src_ref=src.at[entries, theirs],
                 dst_ref=dst.at[entries, mine],
-                send_sem=send_sem.at[chunk],
-                recv_sem=recv_sem.at[chunk],
+                send_sem=send_sem,
+                recv_sem=recv_sem,
                 device_id={"slab": peer},
                 device_id_type=MESH,
             ).start()
 
         dst[entries, mine, :] = src[entries, mine, :]
 
-    def wait_all(ref, chunk, width, sem):
-        part = ref.at[pl.ds(2 * chunk, len(CHUNKS[chunk])), pl.ds(0, (SLABS - 1) * width)]
-        pltpu.make_async_copy(part, part, sem.at[chunk]).wait()
+    def wait_all(ref, number, width, sem):
+        part = ref.at[pl.ds(0, number), pl.ds(0, (SLABS - 1) * width)]
+        pltpu.make_async_copy(part, part, sem).wait()
 
     def turned(value):
         swapped = [
@@ -197,17 +205,39 @@
     def stage_x(chunk):
         for i, slot in enumerate(CHUNKS[chunk]):
             along_x(slot, 2 * chunk + i)
-        exchange(send_a, lines, chunk, PLANES, a_send, a_recv)
+        number = len(CHUNKS[chunk])
+        exchange(
+            send_a, lines, 2 * chunk, number, PLANES, a_send.at[chunk], a_recv.at[chunk]
+        )
 
     def stage_z(chunk):
-        wait_all(lines, chunk, PLANES, a_recv)
-        count_here = len(CHUNKS[chunk])
-        value = jnp.concatenate([lines[2 * chunk + i] for i in range(count_here)], axis=1)
+        number = len(CHUNKS[chunk])
+        first = 2 * chunk
+        wait_all(lines, number, PLANES, a_recv.at[chunk])
+        value = jnp.concatenate([lines[first + i] for i in range(number)], axis=1)
         out = transform(ez, value)
-        for i in range(count_here):
-            send_b[2 * chunk + i] = out[:, i * LANES : (i + 1) * LANES]
-        exchange(send_b, planes, chunk, KZ, b_send, b_recv)
-
+        for i in range(number):
+            send_b[first + i] = out[:, i * LANES : (i + 1) * LANES]
+        if chunk == 4:
+            exchange(
+                send_b, planes, first, number, KZ, b_send.at[chunk], b_recv.at[chunk]
+            )
+            return
+
+        @pl.loop(0, SLABS, unroll=4)
+        def _(owner):
+            rows = pl.ds(pl.multiple_of(owner * KZ, KZ), KZ)
+            for i in range(number):
+                block = send_b[first + i, rows, :]
+                top = jnp.maximum(jnp.max(jnp.abs(block), axis=0, keepdims=True), 1e-30)
+                send_q[first + i, rows, :] = jnp.round(block * (STEPS / top)).astype(jnp.int16)
+                send_s[0, pl.ds(owner * 8 + first + i, 1), :] = top * (1.0 / STEPS)
+
+        exchange(send_q, coded, first, number, KZ, b_send.at[chunk], b_recv.at[chunk])
+        if chunk == 3:
+            exchange(send_s, scales, 0, 1, 8, s_send.at[0], s_recv.at[0])
+
+    send_s[...] = jnp.zeros((1, SLABS * 8, LANES), F32)
     load_img.wait()
     load_maps.wait()
     load_tx.wait()
@@ -218,11 +248,20 @@
         stage_x(chunk)
         stage_z(chunk - 1)
     stage_z(4)
-    load_ey.wait()
-    load_place.wait()
-    load_kern.wait()
-    for chunk in range(5):
-        wait_all(planes, chunk, KZ, b_recv)
+    for copy in late_loads:
+        copy.wait()
+    wait_all(scales, 1, 8, s_recv.at[0])
+    for chunk in range(4):
+        wait_all(coded, len(CHUNKS[chunk]), KZ, b_recv.at[chunk])
+
+    @pl.loop(0, SLABS, unroll=2)
+    def _(source):
+        rows = pl.ds(pl.multiple_of(source * KZ, KZ), KZ)
+        for entry in (0, 2, 3, 4, 5, 6, 7):
+            scale = scales[0, pl.ds(source * 8 + entry, 1), :]
+            planes[entry, rows, :] = coded[entry, rows, :].astype(F32) * scale
+
+    wait_all(planes, 1, KZ, b_recv.at[4])
 
     def entry_of(block):
         slot = lax.rem(block - coil + COILS, COILS)
@@ -246,19 +285,22 @@
 
     place_of = lax.broadcasted_iota(jnp.int32, (8, LANES), 1) // 8
 
-    @pl.loop(0, SLOTS, unroll=4)
-    def _(slot):
-        tile = ids[slot]
-        first = (tile >> 9) * 256 + (tile & 63)
-        b = jnp.full((8, LANES), (tile >> 6) & 7, jnp.int32)
-        away = (place_of - b) & 7
-        total = jnp.zeros((8, LANES), F32)
-        for u in range(4):
-            value = grid[first + 64 * u]
-            total = jnp.where(away == u, pltpu.roll(value, 8 * u, 1) if u else value, total)
-        for bit in (1, 2, 4):
-            total = jnp.where((b & bit) > 0, pltpu.roll(total, LANES - 8 * bit, 1), total)
-        picked[pl.ds(pl.multiple_of(slot * 8, 8), 8), :] = total
+    @pl.loop(0, SLOTS // 8)
+    def _(index):
+        found = []
+        for k in range(8):
+            tile = ids[index * 8 + k]
+            first = (tile >> 9) * 256 + (tile & 63)
+            b = jnp.full((8, LANES), (tile >> 6) & 7, jnp.int32)
+            away = (place_of - b) & 7
+            total = jnp.zeros((8, LANES), F32)
+            for u in range(4):
+                value = grid[first + 64 * u]
+                total = jnp.where(away == u, pltpu.roll(value, 8 * u, 1) if u else value, total)
+            for bit in (1, 2, 4):
+                total = jnp.where((b & bit) > 0, pltpu.roll(total, LANES - 8 * bit, 1), total)
+            found.append(total)
+        picked[pl.ds(pl.multiple_of(index * 64, 64), 64), :] = jnp.concatenate(found, axis=0)
 
     high_sum = jnp.zeros((SLOTS, 512), F32)
     low_sum = jnp.zeros((SLOTS, 512), F32)
@@ -293,7 +335,7 @@
         alive = first + row < live
         for part in range(2):
             predicted = total[16 * part : 16 * part + 8] + total[16 * part + 8 : 16 * part + 16]
-            value = jnp.where(alive, predicted - meas[0, part, rows, :], 0.0)
+            value = jnp.where(alive, predicted - meas[part, rows, :], 0.0)
             res[0, part, rows, :] = value
             squares = squares + value * value
         return squares
@@ -322,13 +364,15 @@
     squares = total_over(sums_s, "slab", me, SLABS, 1, squares)
     total = jnp.sum(jnp.sum(squares, axis=1, keepdims=True), axis=0, keepdims=True)
     root = jnp.sqrt(total * (1.0 / (COILS * 2 * SLABS * SLOTS * LANES)))
-    rms[...] = jnp.broadcast_to(root, (8, LANES))
+    rms[0] = root[0, 0]
 
     for copy in hops.values():
         copy.wait_send()
     for chunk in range(5):
-        wait_all(send_a, chunk, PLANES, a_send)
-        wait_all(send_b, chunk, KZ, b_send)
+        number = len(CHUNKS[chunk])
+        wait_all(send_a, number, PLANES, a_send.at[chunk])
+        wait_all(send_q if chunk < 4 else send_b, number, KZ, b_send.at[chunk])
+    wait_all(send_s, 1, 8, s_send.at[0])
     for which, (buffer, size) in enumerate(((sums_c, COILS), (sums_s, SLABS))):
         others = buffer.at[pl.ds(0, size - 1)]
         pltpu.make_async_copy(others, others, sum_send.at[which]).wait()
@@ -348,14 +392,17 @@
         kernel,
         out_shape=(
             jax.ShapeDtypeStruct((1, 2, SLOTS, LANES), F32),
-            jax.ShapeDtypeStruct((8, LANES), F32),
+            jax.ShapeDtypeStruct((1,), F32),
         ),
-        in_specs=[hbm, hbm, hbm, smem, smem, vmem, hbm, hbm, hbm, hbm],
-        out_specs=(vmem, vmem),
+        in_specs=[hbm] * 10,
+        out_specs=(vmem, smem),
         scratch_shapes=[
             pltpu.VMEM((8, 2, PLANES, YB, IMG), BF16),
             pltpu.VMEM((2, PLANES, IMG, IMG), BF16),
             pltpu.VMEM((SLOTS, LANES, 256), BF16),
+            pltpu.SMEM((SLOTS,), jnp.int32),
+            pltpu.SMEM((1,), jnp.int32),
+            pltpu.VMEM((2, SLOTS, LANES), F32),
             pltpu.VMEM((2 * IMG, 2 * LANES), BF16),
             pltpu.VMEM((FREQ, 6 * IMG), BF16),
             pltpu.VMEM((FREQ, 6 * IMG), BF16),
@@ -364,18 +411,24 @@
             pltpu.VMEM((10, SLABS * PLANES, LANES), F32),
             pltpu.VMEM((10, FREQ, LANES), F32),
             pltpu.VMEM((10, FREQ, LANES), F32),
+            pltpu.VMEM((8, FREQ, LANES), jnp.int16),
+            pltpu.VMEM((8, FREQ, LANES), jnp.int16),
+            pltpu.VMEM((1, SLABS * 8, LANES), F32),
+            pltpu.VMEM((1, SLABS * 8, LANES), F32),
             pltpu.VMEM((KZ * 64, 8, LANES), F32),
             pltpu.VMEM((SLOTS * 8, LANES), F32),
             pltpu.VMEM((2, SLOTS, 512), F32),
             pltpu.VMEM((COILS, 8, LANES), F32),
             pltpu.VMEM((SLABS, 8, LANES), F32),
-            pltpu.SemaphoreType.DMA((7,)),
+            pltpu.SemaphoreType.DMA((10,)),
             pltpu.SemaphoreType.DMA((2, 4, 2)),
             pltpu.SemaphoreType.DMA((2, 4, 2)),
             pltpu.SemaphoreType.DMA((5,)),
             pltpu.SemaphoreType.DMA((5,)),
             pltpu.SemaphoreType.DMA((5,)),
             pltpu.SemaphoreType.DMA((5,)),
+            pltpu.SemaphoreType.DMA((1,)),
+            pltpu.SemaphoreType.DMA((1,)),
             pltpu.SemaphoreType.DMA((2,)),
             pltpu.SemaphoreType.DMA((2,)),
         ],
@@ -386,7 +439,7 @@
             flops=6_000_000_000, bytes_accessed=20_000_000, transcendentals=0
         ),
     )(image_est, coil_maps, kernel_tiles, tile_ids, tile_count, measured, *tables)
-    return residual, rms[0, :1]
+    return residual, rms
 
 
 def solution(mesh):

time: 97.1 us -> 83.8 us (0.86)
  Pallas kernels: 92.9 us -> 79 us
  between operations: 1.29 us -> 3.05 us
  local copies, waits for them, and re-layouts: 2.78 us -> 1.59 us
    pallas_call x1, Pallas kernels: 92.9 us -> 79 us  [per_device(): pl.pallas_call(kernel, out_shape=(jax.ShapeDtypeStruct((1, 2, SLOTS, LANE...]
    slice x1 -> x0, local copies, waits for them, and re-layouts: 1.19 us -> none  [per_device(): return (residual, rms[0, :1])]
where the time goes in v1:
time: 83.8 us; the launch traced here: 83.6 us
  Pallas kernels  79 us (94%)
  between operations  3.05 us (4%)
  local copies, waits for them, and re-layouts  1.59 us (2%)
    pallas_call x1, Pallas kernels, per_device(): pl.pallas_call(kernel, out_shape=(jax.ShapeDtypeStruct((1, 2, SLOTS, LANE...  79 us

profile of v1, /device:TPU:1, one launch (start us, length us, event | category | flops | bytes accessed | tf_op | source)
XLA Modules:
  0.0 83.6 jit_solution(17003534852235700522)
XLA Ops:
  1.3 79.0 %shard_map.113 = (f32[1,2,160,128]{3,2,1,0:T(8,128)}, f32[1]{0:T(128)}) custom-call(bf16[2,8,32,256]{3,2,1,0:T(8,128)(2,1)} %img_hbm.1, bf16[1,2,8,256,256]{4,3,2,1,0:T(8,128)(2,1)} %maps_hbm.1, bf16[160,128,256]{2,1,0:T(8,128)(2,1)} %kern_hbm.1, s32[160]{0:T(256)} %ids_hbm.1, s32[1]{0:T(128)S(6)} %copy.14.count_hbm, f32[1,2,160,128]{3,2,1,0:T(8,128)} %meas_hbm.1, ...), custom_call_target="tpu_custom_call" | custom-call | flops 6000000000 | bytes 20000000 | tf_op jit(solution)/shard_map/pallas_call | solution.py:391
  80.3 1.6 %copy.15 = f32[1,2,160,128]{3,2,1,0:T(8,128)} copy(f32[1,2,160,128]{3,2,1,0:T(8,128)} %get-tuple-element.4) | data formatting | bytes 327680

commit v2 on v1

--- a/solution.py
+++ b/solution.py
@@ -23,6 +23,10 @@
 SLOTS = 160
 STEPS = 32760.0
 CHUNKS = ((0,), (1, 7), (2, 6), (3, 5), (4,))
+FIRST = (0, 1, 3, 5, 7)
+GROUPS = ((0, 1), (1, 3), (3, 5), (5, 9))
+EXPONENTS = 8
+FINE = 16.0
 
 
 def split_table(table):
@@ -71,10 +75,9 @@
     img_hbm, maps_hbm, kern_hbm, ids_hbm, count_hbm, meas_hbm, tx_hbm, ez_hbm, ey_hbm, place_hbm,
     res, rms,
     img, maps, kern, ids, count, meas, tx, ez, ey, place,
-    send_a, lines, send_b, planes, send_q, coded, send_s, scales, grid, picked, cells,
+    send_a, lines, send_b, planes, send_q, coded, power, grid, picked, cells,
     sums_c, sums_s,
-    load_sem, ring_send, ring_recv, a_send, a_recv, b_send, b_recv, s_send, s_recv,
-    sum_send, sum_recv,
+    load_sem, ring_send, ring_recv, a_send, a_recv, b_send, b_recv, sum_send, sum_recv,
 ):
     me = lax.axis_index("slab")
     coil = lax.axis_index("coil")
@@ -204,25 +207,20 @@
 
     def stage_x(chunk):
         for i, slot in enumerate(CHUNKS[chunk]):
-            along_x(slot, 2 * chunk + i)
+            along_x(slot, FIRST[chunk] + i)
         number = len(CHUNKS[chunk])
         exchange(
-            send_a, lines, 2 * chunk, number, PLANES, a_send.at[chunk], a_recv.at[chunk]
+            send_a, lines, FIRST[chunk], number, PLANES, a_send.at[chunk], a_recv.at[chunk]
         )
 
     def stage_z(chunk):
         number = len(CHUNKS[chunk])
-        first = 2 * chunk
+        first = FIRST[chunk]
         wait_all(lines, number, PLANES, a_recv.at[chunk])
         value = jnp.concatenate([lines[first + i] for i in range(number)], axis=1)
         out = transform(ez, value)
         for i in range(number):
             send_b[first + i] = out[:, i * LANES : (i + 1) * LANES]
-        if chunk == 4:
-            exchange(
-                send_b, planes, first, number, KZ, b_send.at[chunk], b_recv.at[chunk]
-            )
-            return
 
         @pl.loop(0, SLABS, unroll=4)
         def _(owner):
@@ -230,42 +228,49 @@
             for i in range(number):
                 block = send_b[first + i, rows, :]
                 top = jnp.maximum(jnp.max(jnp.abs(block), axis=0, keepdims=True), 1e-30)
-                send_q[first + i, rows, :] = jnp.round(block * (STEPS / top)).astype(jnp.int16)
-                send_s[0, pl.ds(owner * 8 + first + i, 1), :] = top * (1.0 / STEPS)
-
-        exchange(send_q, coded, first, number, KZ, b_send.at[chunk], b_recv.at[chunk])
-        if chunk == 3:
-            exchange(send_s, scales, 0, 1, 8, s_send.at[0], s_recv.at[0])
-
-    send_s[...] = jnp.zeros((1, SLABS * 8, LANES), F32)
+                exponent = jnp.ceil(jnp.log2(top) * FINE)
+                factor = jnp.exp2(exponent * (-1.0 / FINE)) * STEPS
+                send_q[first + i, rows, :] = jnp.round(block * factor).astype(jnp.int16)
+                power[pl.ds(owner * KZ + first + i, 1), :] = exponent
+
+    def stage_send(group):
+        start, stop = GROUPS[group]
+        if group == 3:
+            send_q[EXPONENTS] = power[...].astype(jnp.int16)
+        exchange(send_q, coded, start, stop - start, KZ, b_send.at[group], b_recv.at[group])
+
+    power[...] = jnp.zeros((FREQ, LANES), F32)
     load_img.wait()
     load_maps.wait()
     load_tx.wait()
     stage_x(0)
     load_ez.wait()
-    for chunk in range(1, 5):
+    for chunk in range(1, 4):
         arrive(chunk)
         stage_x(chunk)
         stage_z(chunk - 1)
+        stage_send(chunk - 1)
+    arrive(4)
+    stage_x(4)
+    stage_z(3)
     stage_z(4)
+    stage_send(3)
     for copy in late_loads:
         copy.wait()
-    wait_all(scales, 1, 8, s_recv.at[0])
-    for chunk in range(4):
-        wait_all(coded, len(CHUNKS[chunk]), KZ, b_recv.at[chunk])
-
-    @pl.loop(0, SLABS, unroll=2)
+    for group, (start, stop) in enumerate(GROUPS):
+        wait_all(coded, stop - start, KZ, b_recv.at[group])
+    power[...] = jnp.exp2(coded[EXPONENTS].astype(F32) * (1.0 / FINE)) * (1.0 / STEPS)
+
+    @pl.loop(0, SLABS, unroll=4)
     def _(source):
         rows = pl.ds(pl.multiple_of(source * KZ, KZ), KZ)
-        for entry in (0, 2, 3, 4, 5, 6, 7):
-            scale = scales[0, pl.ds(source * 8 + entry, 1), :]
+        for entry in range(8):
+            scale = power[pl.ds(source * KZ + entry, 1), :]
             planes[entry, rows, :] = coded[entry, rows, :].astype(F32) * scale
-
-    wait_all(planes, 1, KZ, b_recv.at[4])
 
     def entry_of(block):
         slot = lax.rem(block - coil + COILS, COILS)
-        return jnp.where(slot <= 4, 2 * slot, 2 * (COILS - slot) + 1)
+        return jnp.where(slot <= 4, jnp.maximum(2 * slot - 1, 0), 2 * (COILS - slot))
 
     entries = [entry_of(block) for block in range(COILS)]
 
@@ -285,11 +290,11 @@
 
     place_of = lax.broadcasted_iota(jnp.int32, (8, LANES), 1) // 8
 
-    @pl.loop(0, SLOTS // 8)
+    @pl.loop(0, SLOTS // 32)
     def _(index):
         found = []
-        for k in range(8):
-            tile = ids[index * 8 + k]
+        for k in range(32):
+            tile = ids[index * 32 + k]
             first = (tile >> 9) * 256 + (tile & 63)
             b = jnp.full((8, LANES), (tile >> 6) & 7, jnp.int32)
             away = (place_of - b) & 7
@@ -300,7 +305,7 @@
             for bit in (1, 2, 4):
                 total = jnp.where((b & bit) > 0, pltpu.roll(total, LANES - 8 * bit, 1), total)
             found.append(total)
-        picked[pl.ds(pl.multiple_of(index * 64, 64), 64), :] = jnp.concatenate(found, axis=0)
+        picked[pl.ds(pl.multiple_of(index * 256, 256), 256), :] = jnp.concatenate(found, axis=0)
 
     high_sum = jnp.zeros((SLOTS, 512), F32)
     low_sum = jnp.zeros((SLOTS, 512), F32)
@@ -327,11 +332,15 @@
             axis=0,
         ).astype(BF16)
         total = jnp.zeros((32, LANES), F32)
-        for s in range(8):
+        for s in range(0, 8, 2):
             product = lax.dot_general(
-                left_side, kern[first + s], (((1,), (1,)), ((), ())), preferred_element_type=F32
+                left_side,
+                kern[pl.ds(first + s, 2)].reshape(2 * LANES, 256),
+                (((1,), (1,)), ((), ())),
+                preferred_element_type=F32,
             )
-            total = jnp.where(row4 == s, product, total)
+            total = jnp.where(row4 == s, product[:, :LANES], total)
+            total = jnp.where(row4 == s + 1, product[:, LANES:], total)
         alive = first + row < live
         for part in range(2):
             predicted = total[16 * part : 16 * part + 8] + total[16 * part + 8 : 16 * part + 16]
@@ -369,10 +378,9 @@
     for copy in hops.values():
         copy.wait_send()
     for chunk in range(5):
-        number = len(CHUNKS[chunk])
-        wait_all(send_a, number, PLANES, a_send.at[chunk])
-        wait_all(send_q if chunk < 4 else send_b, number, KZ, b_send.at[chunk])
-    wait_all(send_s, 1, 8, s_send.at[0])
+        wait_all(send_a, len(CHUNKS[chunk]), PLANES, a_send.at[chunk])
+    for group, (start, stop) in enumerate(GROUPS):
+        wait_all(send_q, stop - start, KZ, b_send.at[group])
     for which, (buffer, size) in enumerate(((sums_c, COILS), (sums_s, SLABS))):
         others = buffer.at[pl.ds(0, size - 1)]
         pltpu.make_async_copy(others, others, sum_send.at[which]).wait()
@@ -391,7 +399,7 @@
     residual, rms = pl.pallas_call(
         kernel,
         out_shape=(
-            jax.ShapeDtypeStruct((1, 2, SLOTS, LANES), F32),
+            pltpu.VMEM((1, 2, SLOTS, LANES), F32),
             jax.ShapeDtypeStruct((1,), F32),
         ),
         in_specs=[hbm] * 10,
@@ -407,14 +415,13 @@
             pltpu.VMEM((FREQ, 6 * IMG), BF16),
             pltpu.VMEM((FREQ, 6 * IMG), BF16),
             pltpu.VMEM((1024, 512), BF16),
-            pltpu.VMEM((10, SLABS * PLANES, LANES), F32),
-            pltpu.VMEM((10, SLABS * PLANES, LANES), F32),
-            pltpu.VMEM((10, FREQ, LANES), F32),
-            pltpu.VMEM((10, FREQ, LANES), F32),
-            pltpu.VMEM((8, FREQ, LANES), jnp.int16),
-            pltpu.VMEM((8, FREQ, LANES), jnp.int16),
-            pltpu.VMEM((1, SLABS * 8, LANES), F32),
-            pltpu.VMEM((1, SLABS * 8, LANES), F32),
+            pltpu.VMEM((8, SLABS * PLANES, LANES), F32),
+            pltpu.VMEM((8, SLABS * PLANES, LANES), F32),
+            pltpu.VMEM((8, FREQ, LANES), F32),
+            pltpu.VMEM((8, FREQ, LANES), F32),
+            pltpu.VMEM((9, FREQ, LANES), jnp.int16),
+            pltpu.VMEM((9, FREQ, LANES), jnp.int16),
+            pltpu.VMEM((FREQ, LANES), F32),
             pltpu.VMEM((KZ * 64, 8, LANES), F32),
             pltpu.VMEM((SLOTS * 8, LANES), F32),
             pltpu.VMEM((2, SLOTS, 512), F32),
@@ -425,10 +432,8 @@
             pltpu.SemaphoreType.DMA((2, 4, 2)),
             pltpu.SemaphoreType.DMA((5,)),
             pltpu.SemaphoreType.DMA((5,)),
-            pltpu.SemaphoreType.DMA((5,)),
-            pltpu.SemaphoreType.DMA((5,)),
-            pltpu.SemaphoreType.DMA((1,)),
-            pltpu.SemaphoreType.DMA((1,)),
+            pltpu.SemaphoreType.DMA((4,)),
+            pltpu.SemaphoreType.DMA((4,)),
             pltpu.SemaphoreType.DMA((2,)),
             pltpu.SemaphoreType.DMA((2,)),
         ],

time: 83.8 us -> 81.6 us (0.974)
  Pallas kernels: 79 us -> 77.8 us
  local copies, waits for them, and re-layouts: 1.59 us -> 0.67 us
    pallas_call x1, Pallas kernels: 79 us -> 77.8 us  [per_device(): pl.pallas_call(kernel, out_shape=(pltpu.VMEM((1, 2, SLOTS, LANES), F32),...]
    unnamed x1, local copies, waits for them, and re-layouts: 1.59 us -> 0.67 us
where the time goes in v2:
time: 81.6 us; the launch traced here: 81.5 us
  Pallas kernels  77.8 us (95%)
  between operations  2.97 us (4%)
    pallas_call x1, Pallas kernels, per_device(): pl.pallas_call(kernel, out_shape=(pltpu.VMEM((1, 2, SLOTS, LANES), F32),...  77.8 us

profile of v2, /device:TPU:1, one launch (start us, length us, event | category | flops | bytes accessed | tf_op | source)
XLA Modules:
  0.0 81.5 jit_solution(13113637511264291188)
XLA Ops:
  1.3 77.8 %shard_map.113 = (f32[1,2,160,128]{3,2,1,0:T(8,128)S(1)}, f32[1]{0:T(128)}) custom-call(bf16[2,8,32,256]{3,2,1,0:T(8,128)(2,1)} %img_hbm.1, bf16[1,2,8,256,256]{4,3,2,1,0:T(8,128)(2,1)} %maps_hbm.1, bf16[160,128,256]{2,1,0:T(8,128)(2,1)} %kern_hbm.1, s32[160]{0:T(256)} %ids_hbm.1, s32[1]{0:T(128)S(6)} %copy.15.count_hbm, f32[1,2,160,128]{3,2,1,0:T(8,128)} %meas_hbm.1, ...), custom_call_target="tpu_custom_call" | custom-call | flops 6000000000 | bytes 20000000 | tf_op jit(solution)/shard_map/pallas_call | solution.py:399
  79.1 0.7 copy.14

commit v3 on v2

--- a/solution.py
+++ b/solution.py
@@ -22,10 +22,12 @@
 KZ = 16
 SLOTS = 160
 STEPS = 32760.0
-CHUNKS = ((0,), (1, 7), (2, 6), (3, 5), (4,))
-FIRST = (0, 1, 3, 5, 7)
-GROUPS = ((0, 1), (1, 3), (3, 5), (5, 9))
-EXPONENTS = 8
+CHUNKS = ((0, 1, 7), (2, 6), (3, 5), (4,))
+FIRST = (0, 3, 5, 7)
+ORDER = (0, 1, 7, 2, 6, 3, 5, 4)
+GROUPS = ((0, 4), (4, 7), (7, 11))
+MEMBERS = ((0, 1, 2), (3, 4), (5, 6, 7))
+ENTRY = (0, 1, 2, 4, 5, 7, 8, 9)
 FINE = 16.0
 
 
@@ -53,6 +55,21 @@
     phase = angles(FREQ, IMG, row_offset, col_offset)
     high, low = split_table(np.concatenate([np.cos(phase), np.sin(phase)], axis=1))
     return np.concatenate([high, high, low], axis=1)
+
+
+def y_table():
+    phase = angles(FREQ, IMG, FREQ // 2, IMG // 2)
+    cosine, sine = np.cos(phase), np.sin(phase)
+    tables = []
+    for coil in range(COILS):
+        parts = []
+        for half in range(2):
+            blocks = [(coil + slot) % COILS for slot in ORDER[4 * half : 4 * half + 4]]
+            columns = np.concatenate([np.arange(YB) + YB * block for block in blocks])
+            high, low = split_table(np.concatenate([cosine[:, columns], sine[:, columns]], axis=1))
+            parts += [high, low]
+        tables.append(np.concatenate(parts, axis=1))
+    return np.stack(tables)
 
 
 def place_table():
@@ -75,8 +92,8 @@
     img_hbm, maps_hbm, kern_hbm, ids_hbm, count_hbm, meas_hbm, tx_hbm, ez_hbm, ey_hbm, place_hbm,
     res, rms,
     img, maps, kern, ids, count, meas, tx, ez, ey, place,
-    send_a, lines, send_b, planes, send_q, coded, power, grid, picked, cells,
-    sums_c, sums_s,
+    send_a, lines, send_b, planes, send_q, coded, power, scale, grid, picked, cells,
+    sums_x, sums_y, sums_z,
     load_sem, ring_send, ring_recv, a_send, a_recv, b_send, b_recv, sum_send, sum_recv,
 ):
     me = lax.axis_index("slab")
@@ -135,7 +152,7 @@
 
     load_ez = load(3, ez_hbm, ez)
     late_loads = [
-        load(4, ey_hbm, ey),
+        load(4, ey_hbm.at[coil], ey),
         load(5, place_hbm, place),
         load(6, kern_hbm, kern),
         load(7, ids_hbm, ids),
@@ -199,6 +216,14 @@
         ]
         return jnp.concatenate([value, jnp.concatenate(swapped, axis=1)], axis=0)
 
+    def transform_half(half, value):
+        high, low = split(turned(value))
+        table_high = ey[:, 512 * half : 512 * half + 256]
+        table_low = ey[:, 512 * half + 256 : 512 * half + 512]
+        out = jnp.dot(table_high, high, preferred_element_type=F32)
+        out = out + jnp.dot(table_high, low, preferred_element_type=F32)
+        return out + jnp.dot(table_low, high, preferred_element_type=F32)
+
     def transform(table, value):
         high, low = split(turned(value))
         return jnp.dot(
@@ -207,7 +232,8 @@
 
     def stage_x(chunk):
         for i, slot in enumerate(CHUNKS[chunk]):
-            along_x(slot, FIRST[chunk] + i)
+            if slot:
+                along_x(slot, FIRST[chunk] + i)
         number = len(CHUNKS[chunk])
         exchange(
             send_a, lines, FIRST[chunk], number, PLANES, a_send.at[chunk], a_recv.at[chunk]
@@ -230,63 +256,74 @@
                 top = jnp.maximum(jnp.max(jnp.abs(block), axis=0, keepdims=True), 1e-30)
                 exponent = jnp.ceil(jnp.log2(top) * FINE)
                 factor = jnp.exp2(exponent * (-1.0 / FINE)) * STEPS
-                send_q[first + i, rows, :] = jnp.round(block * factor).astype(jnp.int16)
+                send_q[ENTRY[first + i], rows, :] = jnp.round(block * factor).astype(jnp.int16)
                 power[pl.ds(owner * KZ + first + i, 1), :] = exponent
 
     def stage_send(group):
         start, stop = GROUPS[group]
-        if group == 3:
-            send_q[EXPONENTS] = power[...].astype(jnp.int16)
+        send_q[stop - 1] = power[...].astype(jnp.int16)
         exchange(send_q, coded, start, stop - start, KZ, b_send.at[group], b_recv.at[group])
 
     power[...] = jnp.zeros((FREQ, LANES), F32)
     load_img.wait()
     load_maps.wait()
     load_tx.wait()
+    along_x(0, 0)
+    load_ez.wait()
+    arrive(1)
     stage_x(0)
-    load_ez.wait()
-    for chunk in range(1, 4):
-        arrive(chunk)
-        stage_x(chunk)
-        stage_z(chunk - 1)
-        stage_send(chunk - 1)
+    arrive(2)
+    stage_x(1)
+    stage_z(0)
+    stage_send(0)
+    arrive(3)
+    stage_x(2)
     arrive(4)
-    stage_x(4)
+    stage_x(3)
+    stage_z(1)
+    stage_send(1)
+    stage_z(2)
     stage_z(3)
-    stage_z(4)
-    stage_send(3)
+    stage_send(2)
     for copy in late_loads:
         copy.wait()
-    for group, (start, stop) in enumerate(GROUPS):
+
+    def decode(group):
+        start, stop = GROUPS[group]
         wait_all(coded, stop - start, KZ, b_recv.at[group])
-    power[...] = jnp.exp2(coded[EXPONENTS].astype(F32) * (1.0 / FINE)) * (1.0 / STEPS)
-
-    @pl.loop(0, SLABS, unroll=4)
-    def _(source):
-        rows = pl.ds(pl.multiple_of(source * KZ, KZ), KZ)
-        for entry in range(8):
-            scale = power[pl.ds(source * KZ + entry, 1), :]
-            planes[entry, rows, :] = coded[entry, rows, :].astype(F32) * scale
-
-    def entry_of(block):
-        slot = lax.rem(block - coil + COILS, COILS)
-        return jnp.where(slot <= 4, jnp.maximum(2 * slot - 1, 0), 2 * (COILS - slot))
-
-    entries = [entry_of(block) for block in range(COILS)]
-
-    @pl.loop(0, KZ // 2)
-    def _(pair):
-        halves = []
-        for odd in range(2):
-            halves.append(
-                jnp.concatenate(
-                    [planes[e, pl.ds(2 * pair + odd, SLABS, stride=KZ), :] for e in entries], axis=0
+        scale[...] = jnp.exp2(coded[stop - 1].astype(F32) * (1.0 / FINE)) * (1.0 / STEPS)
+
+        @pl.loop(0, SLABS, unroll=4)
+        def _(source):
+            rows = pl.ds(pl.multiple_of(source * KZ, KZ), KZ)
+            for member in MEMBERS[group]:
+                factor = scale[pl.ds(source * KZ + member, 1), :]
+                planes[member, rows, :] = coded[ENTRY[member], rows, :].astype(F32) * factor
+
+    def along_y(half):
+        @pl.loop(0, KZ // 2)
+        def _(pair):
+            sides = []
+            for odd in range(2):
+                rows = pl.ds(2 * pair + odd, SLABS, stride=KZ)
+                sides.append(
+                    jnp.concatenate(
+                        [planes[4 * half + i, rows, :] for i in range(4)], axis=0
+                    )
                 )
-            )
-        out = transform(ey, jnp.concatenate(halves, axis=1))
-        for odd in range(2):
-            half = out[:, odd * LANES : (odd + 1) * LANES].reshape(64, 8, LANES)
-            grid[pl.ds((2 * pair + odd) * 64, 64)] = half
+            out = transform_half(half, jnp.concatenate(sides, axis=1))
+            for odd in range(2):
+                side = out[:, odd * LANES : (odd + 1) * LANES].reshape(64, 8, LANES)
+                place_here = pl.ds((2 * pair + odd) * 64, 64)
+                if half:
+                    side = side + grid[place_here]
+                grid[place_here] = side
+
+    decode(0)
+    decode(1)
+    along_y(0)
+    decode(2)
+    along_y(1)
 
     place_of = lax.broadcasted_iota(jnp.int32, (8, LANES), 1) // 8
 
@@ -351,7 +388,7 @@
 
     squares = lax.fori_loop(0, SLOTS // 8, degrid, jnp.zeros((8, LANES), F32))
 
-    def total_over(buffer, axis, position, size, which, value):
+    def total_over(which, buffer, size, position, axis, peer_of, value):
         buffer[position] = value
 
         @pl.loop(1, size)
@@ -361,7 +398,7 @@
                 dst_ref=buffer.at[position],
                 send_sem=sum_send.at[which],
                 recv_sem=sum_recv.at[which],
-                device_id={axis: lax.rem(position + step, size)},
+                device_id={axis: peer_of(lax.rem(position + step, size))},
                 device_id_type=MESH,
             ).start()
 
@@ -369,19 +406,25 @@
         pltpu.make_async_copy(others, others, sum_recv.at[which]).wait()
         return jnp.sum(buffer[...], axis=0)
 
-    squares = total_over(sums_c, "coil", coil, COILS, 0, squares)
-    squares = total_over(sums_s, "slab", me, SLABS, 1, squares)
+    inner, outer = lax.rem(me, 8), me // 8
+    rounds = (
+        (sums_x, 8, inner, "slab", lambda k: outer * 8 + k),
+        (sums_y, 4, outer, "slab", lambda k: k * 8 + inner),
+        (sums_z, COILS, coil, "coil", lambda k: k),
+    )
+    for which, (buffer, size, position, axis, peer_of) in enumerate(rounds):
+        squares = total_over(which, buffer, size, position, axis, peer_of, squares)
     total = jnp.sum(jnp.sum(squares, axis=1, keepdims=True), axis=0, keepdims=True)
     root = jnp.sqrt(total * (1.0 / (COILS * 2 * SLABS * SLOTS * LANES)))
     rms[0] = root[0, 0]
 
     for copy in hops.values():
         copy.wait_send()
-    for chunk in range(5):
+    for chunk in range(len(CHUNKS)):
         wait_all(send_a, len(CHUNKS[chunk]), PLANES, a_send.at[chunk])
     for group, (start, stop) in enumerate(GROUPS):
         wait_all(send_q, stop - start, KZ, b_send.at[group])
-    for which, (buffer, size) in enumerate(((sums_c, COILS), (sums_s, SLABS))):
+    for which, (buffer, size, *_) in enumerate(rounds):
         others = buffer.at[pl.ds(0, size - 1)]
         pltpu.make_async_copy(others, others, sum_send.at[which]).wait()
 
@@ -393,7 +436,7 @@
     tables = [
         jnp.asarray(x_table()),
         jnp.asarray(long_table(0, 0)),
-        jnp.asarray(long_table(FREQ // 2, IMG // 2)),
+        jnp.asarray(y_table()),
         jnp.asarray(place_table()),
     ]
     residual, rms = pl.pallas_call(
@@ -413,29 +456,31 @@
             pltpu.VMEM((2, SLOTS, LANES), F32),
             pltpu.VMEM((2 * IMG, 2 * LANES), BF16),
             pltpu.VMEM((FREQ, 6 * IMG), BF16),
-            pltpu.VMEM((FREQ, 6 * IMG), BF16),
+            pltpu.VMEM((FREQ, 4 * IMG), BF16),
             pltpu.VMEM((1024, 512), BF16),
             pltpu.VMEM((8, SLABS * PLANES, LANES), F32),
             pltpu.VMEM((8, SLABS * PLANES, LANES), F32),
             pltpu.VMEM((8, FREQ, LANES), F32),
             pltpu.VMEM((8, FREQ, LANES), F32),
-            pltpu.VMEM((9, FREQ, LANES), jnp.int16),
-            pltpu.VMEM((9, FREQ, LANES), jnp.int16),
+            pltpu.VMEM((11, FREQ, LANES), jnp.int16),
+            pltpu.VMEM((11, FREQ, LANES), jnp.int16),
+            pltpu.VMEM((FREQ, LANES), F32),
             pltpu.VMEM((FREQ, LANES), F32),
             pltpu.VMEM((KZ * 64, 8, LANES), F32),
             pltpu.VMEM((SLOTS * 8, LANES), F32),
             pltpu.VMEM((2, SLOTS, 512), F32),
+            pltpu.VMEM((8, 8, LANES), F32),
+            pltpu.VMEM((4, 8, LANES), F32),
             pltpu.VMEM((COILS, 8, LANES), F32),
-            pltpu.VMEM((SLABS, 8, LANES), F32),
             pltpu.SemaphoreType.DMA((10,)),
             pltpu.SemaphoreType.DMA((2, 4, 2)),
             pltpu.SemaphoreType.DMA((2, 4, 2)),
-            pltpu.SemaphoreType.DMA((5,)),
-            pltpu.SemaphoreType.DMA((5,)),
             pltpu.SemaphoreType.DMA((4,)),
             pltpu.SemaphoreType.DMA((4,)),
-            pltpu.SemaphoreType.DMA((2,)),
-            pltpu.SemaphoreType.DMA((2,)),
+            pltpu.SemaphoreType.DMA((3,)),
+            pltpu.SemaphoreType.DMA((3,)),
+            pltpu.SemaphoreType.DMA((3,)),
+            pltpu.SemaphoreType.DMA((3,)),
         ],
         compiler_params=pltpu.CompilerParams(
             collective_id=0, has_side_effects=True, vmem_limit_bytes=56 * 1024 * 1024

time: 81.6 us -> 80.5 us (0.987)
  Pallas kernels: 77.8 us -> 76.7 us
    pallas_call x1, Pallas kernels: 77.8 us -> 76.7 us  [per_device(): pl.pallas_call(kernel, out_shape=(pltpu.VMEM((1, 2, SLOTS, LANES), F32),...]
where the time goes in v3:
time: 80.5 us; the launch traced here: 80.3 us
  Pallas kernels  76.7 us (95%)
  between operations  2.97 us (4%)
    pallas_call x1, Pallas kernels, per_device(): pl.pallas_call(kernel, out_shape=(pltpu.VMEM((1, 2, SLOTS, LANES), F32),...  76.7 us

profile of v3, /device:TPU:1, one launch (start us, length us, event | category | flops | bytes accessed | tf_op | source)
XLA Modules:
  0.0 80.3 jit_solution(17250064625441560875)
XLA Ops:
  1.3 76.7 %shard_map.113 = (f32[1,2,160,128]{3,2,1,0:T(8,128)S(1)}, f32[1]{0:T(128)}) custom-call(bf16[2,8,32,256]{3,2,1,0:T(8,128)(2,1)} %img_hbm.1, bf16[1,2,8,256,256]{4,3,2,1,0:T(8,128)(2,1)} %maps_hbm.1, bf16[160,128,256]{2,1,0:T(8,128)(2,1)} %kern_hbm.1, s32[160]{0:T(256)} %ids_hbm.1, s32[1]{0:T(128)S(6)} %copy.15.count_hbm, f32[1,2,160,128]{3,2,1,0:T(8,128)} %meas_hbm.1, ...), custom_call_target="tpu_custom_call" | custom-call | flops 6000000000 | bytes 20000000 | tf_op jit(solution)/shard_map/pallas_call | solution.py:442
  78.0 0.7 copy.14

commit v4 on v3

--- a/solution.py
+++ b/solution.py
@@ -248,7 +248,7 @@
         for i in range(number):
             send_b[first + i] = out[:, i * LANES : (i + 1) * LANES]
 
-        @pl.loop(0, SLABS, unroll=4)
+        @pl.loop(0, SLABS, unroll=8)
         def _(owner):
             rows = pl.ds(pl.multiple_of(owner * KZ, KZ), KZ)
             for i in range(number):
@@ -293,7 +293,7 @@
         wait_all(coded, stop - start, KZ, b_recv.at[group])
         scale[...] = jnp.exp2(coded[stop - 1].astype(F32) * (1.0 / FINE)) * (1.0 / STEPS)
 
-        @pl.loop(0, SLABS, unroll=4)
+        @pl.loop(0, SLABS, unroll=8)
         def _(source):
             rows = pl.ds(pl.multiple_of(source * KZ, KZ), KZ)
             for member in MEMBERS[group]:
@@ -301,7 +301,7 @@
                 planes[member, rows, :] = coded[ENTRY[member], rows, :].astype(F32) * factor
 
     def along_y(half):
-        @pl.loop(0, KZ // 2)
+        @pl.loop(0, KZ // 2, unroll=4)
         def _(pair):
             sides = []
             for odd in range(2):
@@ -327,7 +327,7 @@
 
     place_of = lax.broadcasted_iota(jnp.int32, (8, LANES), 1) // 8
 
-    @pl.loop(0, SLOTS // 32)
+    @pl.loop(0, SLOTS // 32, unroll=5)
     def _(index):
         found = []
         for k in range(32):
@@ -386,7 +386,7 @@
             squares = squares + value * value
         return squares
 
-    squares = lax.fori_loop(0, SLOTS // 8, degrid, jnp.zeros((8, LANES), F32))
+    squares = lax.fori_loop(0, SLOTS // 8, degrid, jnp.zeros((8, LANES), F32), unroll=10)
 
     def total_over(which, buffer, size, position, axis, peer_of, value):
         buffer[position] = value

time: 80.5 us -> 76.2 us (0.947)
  Pallas kernels: 76.7 us -> 72.5 us
    pallas_call x1, Pallas kernels: 76.7 us -> 72.5 us  [per_device(): pl.pallas_call(kernel, out_shape=(pltpu.VMEM((1, 2, SLOTS, LANES), F32),...]
where the time goes in v4:
time: 76.2 us; the launch traced here: 76.1 us
  Pallas kernels  72.5 us (95%)
  between operations  2.97 us (4%)
    pallas_call x1, Pallas kernels, per_device(): pl.pallas_call(kernel, out_shape=(pltpu.VMEM((1, 2, SLOTS, LANES), F32),...  72.5 us

profile of v4, /device:TPU:1, one launch (start us, length us, event | category | flops | bytes accessed | tf_op | source)
XLA Modules:
  0.0 76.1 jit_solution(9858922205716547950)
XLA Ops:
  1.3 72.5 %shard_map.113 = (f32[1,2,160,128]{3,2,1,0:T(8,128)S(1)}, f32[1]{0:T(128)}) custom-call(bf16[2,8,32,256]{3,2,1,0:T(8,128)(2,1)} %img_hbm.1, bf16[1,2,8,256,256]{4,3,2,1,0:T(8,128)(2,1)} %maps_hbm.1, bf16[160,128,256]{2,1,0:T(8,128)(2,1)} %kern_hbm.1, s32[160]{0:T(256)} %ids_hbm.1, s32[1]{0:T(128)S(6)} %copy.15.count_hbm, f32[1,2,160,128]{3,2,1,0:T(8,128)} %meas_hbm.1, ...), custom_call_target="tpu_custom_call" | custom-call | flops 6000000000 | bytes 20000000 | tf_op jit(solution)/shard_map/pallas_call | solution.py:442
  73.7 0.7 copy.14

commit v5 on v4

--- a/solution.py
+++ b/solution.py
@@ -93,7 +93,7 @@
     res, rms,
     img, maps, kern, ids, count, meas, tx, ez, ey, place,
     send_a, lines, send_b, planes, send_q, coded, power, scale, grid, picked, cells,
-    sums_x, sums_y, sums_z,
+    sums_z, sums_s,
     load_sem, ring_send, ring_recv, a_send, a_recv, b_send, b_recv, sum_send, sum_recv,
 ):
     me = lax.axis_index("slab")
@@ -406,11 +406,9 @@
         pltpu.make_async_copy(others, others, sum_recv.at[which]).wait()
         return jnp.sum(buffer[...], axis=0)
 
-    inner, outer = lax.rem(me, 8), me // 8
     rounds = (
-        (sums_x, 8, inner, "slab", lambda k: outer * 8 + k),
-        (sums_y, 4, outer, "slab", lambda k: k * 8 + inner),
         (sums_z, COILS, coil, "coil", lambda k: k),
+        (sums_s, SLABS, me, "slab", lambda k: k),
     )
     for which, (buffer, size, position, axis, peer_of) in enumerate(rounds):
         squares = total_over(which, buffer, size, position, axis, peer_of, squares)
@@ -469,9 +467,8 @@
             pltpu.VMEM((KZ * 64, 8, LANES), F32),
             pltpu.VMEM((SLOTS * 8, LANES), F32),
             pltpu.VMEM((2, SLOTS, 512), F32),
-            pltpu.VMEM((8, 8, LANES), F32),
-            pltpu.VMEM((4, 8, LANES), F32),
             pltpu.VMEM((COILS, 8, LANES), F32),
+            pltpu.VMEM((SLABS, 8, LANES), F32),
             pltpu.SemaphoreType.DMA((10,)),
             pltpu.SemaphoreType.DMA((2, 4, 2)),
             pltpu.SemaphoreType.DMA((2, 4, 2)),
@@ -479,8 +476,8 @@
             pltpu.SemaphoreType.DMA((4,)),
             pltpu.SemaphoreType.DMA((3,)),
             pltpu.SemaphoreType.DMA((3,)),
-            pltpu.SemaphoreType.DMA((3,)),
-            pltpu.SemaphoreType.DMA((3,)),
+            pltpu.SemaphoreType.DMA((2,)),
+            pltpu.SemaphoreType.DMA((2,)),
         ],
         compiler_params=pltpu.CompilerParams(
             collective_id=0, has_side_effects=True, vmem_limit_bytes=56 * 1024 * 1024

time: 76.2 us -> 75.8 us (level)
  no operation moved by 1% of the time
where the time goes in v5:
time: 75.8 us; the launch traced here: 75.7 us
  Pallas kernels  72 us (95%)
  between operations  2.97 us (4%)
    pallas_call x1, Pallas kernels, per_device(): pl.pallas_call(kernel, out_shape=(pltpu.VMEM((1, 2, SLOTS, LANES), F32),...  72 us

profile of v5, /device:TPU:1, one launch (start us, length us, event | category | flops | bytes accessed | tf_op | source)
XLA Modules:
  0.0 75.7 jit_solution(4530113014872047005)
XLA Ops:
  1.3 72.0 %shard_map.113 = (f32[1,2,160,128]{3,2,1,0:T(8,128)S(1)}, f32[1]{0:T(128)}) custom-call(bf16[2,8,32,256]{3,2,1,0:T(8,128)(2,1)} %img_hbm.1, bf16[1,2,8,256,256]{4,3,2,1,0:T(8,128)(2,1)} %maps_hbm.1, bf16[160,128,256]{2,1,0:T(8,128)(2,1)} %kern_hbm.1, s32[160]{0:T(256)} %ids_hbm.1, s32[1]{0:T(128)S(6)} %copy.15.count_hbm, f32[1,2,160,128]{3,2,1,0:T(8,128)} %meas_hbm.1, ...), custom_call_target="tpu_custom_call" | custom-call | flops 6000000000 | bytes 20000000 | tf_op jit(solution)/shard_map/pallas_call | solution.py:440
  73.3 0.7 copy.14
